TPU v7x, 32 devices: a whole 2x2x4 slice. The times are simulated.
32 devices in a mesh: comp: 2 (over y), ty: 4 (over z), tx: 4 (over x, core).
Axes of the slice: x: 2, y: 2, z: 4, core: 2. Of those that a mesh axis runs over, the one named last changes fastest.
Arguments:
- ocean: float32 [3, 64, 1024], P(None, 'ty', 'tx'), may hold values from -4 to 4
- tracers: float32 [19, 4, 16, 1024], P(None, 'ty', 'comp', 'tx'), may hold values from 0.05 to 3
- bottom: int32 [64, 16], P('ty', 'tx'), may hold values from 0 to 64, as said below
- stoich: float32 [14], replicated, may hold values from -3 to 3
Outputs:
- ocean_out: float32 [3, 64, 1024], P(None, 'ty', 'tx')
- tracers_out: float32 [19, 4, 16, 1024], P(None, 'ty', 'comp', 'tx')
Inputs may be any that keep to these rules, and one draw needn't show every extreme that they name: bottom counts wet levels from the surface; 0 marks land, 64 a full column.
All inputs are finite; a program needn't handle non-finite values.
Results may differ from a plain program's by a relative error of at most 0.0003.
Values sent between devices are 32-bit elements; how exact they have to be, the bound alone decides.
A program may use at most 64 MiB of HBM per device.

v0:
```python
import jax
import jax.numpy as jnp
from jax import lax
from jax.sharding import PartitionSpec as P

LEV = 64
STEPS = 2


ATTEN_WATER = 0.04
ATTEN_CHL = 0.03
PRESSURE = 0.05
TIME_STEP = 0.2
CORIOLIS = 1.0
DAMPING = 0.05
HEAT_GAIN = 2.0
DIFFUSE = 0.2
ADVECT = 0.08
GROWTH = 1.0
HALF_LIGHT = 0.2
HALF_NUTRIENT = 0.5
TEMP_COEF = 0.1
GRAZE = 0.8
HALF_PREY = 0.3
MORTAL = 0.1
REMIN = 0.2
CHL_RELAX = 0.3
CHL_RATIO = 0.5
CHL_GAIN = 0.2
ASSIM = 0.3
GRAZER_LOSS = 0.05
REACT_STEP = 0.2


def extended_2(cells, sides, width, closed):
    for axis, dim in sides:
        count = lax.axis_size(axis)
        ends = count if closed else count - 1
        head = lax.slice_in_dim(cells, 0, width, axis=dim)
        tail = lax.slice_in_dim(cells, cells.shape[dim] - width, cells.shape[dim], axis=dim)
        cells = jnp.concatenate(
            [
                lax.ppermute(tail, axis, [(i, (i + 1) % count) for i in range(ends)]),
                cells,
                lax.ppermute(head, axis, [((i + 1) % count, i) for i in range(ends)]),
            ],
            axis=dim,
        )
    return cells


def level_sums(values, inclusive):
    count = values.shape[-1]
    level_ids = jnp.arange(count)
    if inclusive:
        ladder = level_ids[:, None] <= level_ids[None, :]
    else:
        ladder = level_ids[:, None] < level_ids[None, :]
    return jnp.dot(values, ladder.astype(jnp.float32), precision=lax.Precision.HIGHEST)


def optics(chloro, wet_mask):
    absorb = (ATTEN_WATER + ATTEN_CHL * jnp.maximum(chloro, 0.0)) * wet_mask
    sunlight = jnp.exp(-level_sums(absorb, False))
    heating = sunlight * (1.0 - jnp.exp(-absorb)) * wet_mask
    return (sunlight, heating)


def ocean_update(current, row_margin, column_margin, heating, wet_mask):
    east = current[0]
    north = current[1]
    temper = current[2]
    press_rows = PRESSURE * level_sums(row_margin, True)
    press_cols = PRESSURE * level_sums(column_margin, True)
    slope_x = 0.5 * (press_cols[:, 2:] - press_cols[:, :-2])
    slope_y = 0.5 * (press_rows[2:] - press_rows[:-2])
    spread = (
        row_margin[2:]
        + row_margin[:-2]
        + column_margin[:, 2:]
        + column_margin[:, :-2]
        - 4.0 * temper
    )
    new_east = wet_mask * ((1.0 - DAMPING) * east + TIME_STEP * (CORIOLIS * north - slope_x))
    new_north = wet_mask * ((1.0 - DAMPING) * north - TIME_STEP * (CORIOLIS * east + slope_y))
    new_temp = wet_mask * (temper + TIME_STEP * (HEAT_GAIN * heating + DIFFUSE * spread))
    return jnp.stack([new_east, new_north, new_temp])


def minmod(first, second):
    return jnp.where(
        first * second > 0.0, jnp.sign(first) * jnp.minimum(jnp.abs(first), jnp.abs(second)), 0.0
    )


def face_transport(field_wide, speed_wide, wet_wide, along_dim, cell_count):

    def window(values, offset):
        return lax.slice_in_dim(values, offset, offset + cell_count + 1, axis=along_dim)

    far_left = window(field_wide, 0)
    left_cell = window(field_wide, 1)
    right_cell = window(field_wide, 2)
    far_right = window(field_wide, 3)
    speed = (
        0.5
        * (window(speed_wide, 1) + window(speed_wide, 2))
        * window(wet_wide, 1)
        * window(wet_wide, 2)
    )
    from_left = left_cell + 0.5 * minmod(left_cell - far_left, right_cell - left_cell)
    from_right = right_cell - 0.5 * minmod(right_cell - left_cell, far_right - right_cell)
    flux = ADVECT * speed * jnp.where(speed > 0.0, from_left, from_right)
    return lax.slice_in_dim(flux, 1, cell_count + 1, axis=along_dim) - lax.slice_in_dim(
        flux, 0, cell_count, axis=along_dim
    )


def reactions(advected, sunlight, temper, stoich, wet_mask):
    nutrient = jnp.maximum(advected[0], 0.0)
    phyto = jnp.maximum(advected[1], 0.0)
    chloro = jnp.maximum(advected[2], 0.0)
    grazer = jnp.maximum(advected[3], 0.0)
    detritus = jnp.maximum(advected[4], 0.0)
    uptake = (
        GROWTH
        * sunlight
        / (sunlight + HALF_LIGHT)
        * nutrient
        / (nutrient + HALF_NUTRIENT)
        * jnp.exp(TEMP_COEF * temper)
    )
    growth = uptake * phyto
    grazing = GRAZE * grazer * phyto * phyto / (phyto * phyto + HALF_PREY)
    dying = MORTAL * phyto
    remineral = REMIN * detritus
    core = jnp.stack(
        [
            remineral - growth,
            growth - grazing - dying,
            CHL_RELAX * (CHL_RATIO * phyto - chloro) + CHL_GAIN * growth,
            ASSIM * grazing - GRAZER_LOSS * grazer,
            dying + (1.0 - ASSIM) * grazing + GRAZER_LOSS * grazer - remineral,
        ]
    )
    others = stoich.reshape((stoich.shape[0],) + (1,) * growth.ndim) * (growth - remineral)[None]
    change_all = jnp.concatenate([core, others], axis=0)
    return (advected + REACT_STEP * change_all) * wet_mask[None]


def edge_bands(values):
    return extended_2(values, (("ty", 1),), 1, False)


def edge_columns(values, rim_width):
    return extended_2(values, (("tx", 2),), rim_width, False)


def neighbour_rows(values, rim_width, group_id, group_count):
    extended = extended_2(values, (("comp", 1),), rim_width, True)
    lower_side = extended[:, :rim_width]
    upper_side = extended[:, -rim_width:]
    handed = jnp.where(group_id == 0, lower_side, upper_side)[:, None]
    beyond = edge_bands(handed)
    lower_side = jnp.where(group_id == 0, beyond[:, 0], lower_side)
    upper_side = jnp.where(group_id == group_count - 1, beyond[:, 2], upper_side)
    return (lower_side, upper_side)


def shards(ocean, tracers, bottom, stoich):
    group_count = lax.axis_size("comp")
    group_id = lax.axis_index("comp")
    num_tracers = tracers.shape[0]
    sub_rows = tracers.shape[2]
    flat_width = tracers.shape[3]
    levels = LEV
    columns = flat_width // levels
    band_rows = ocean.shape[1]
    level_ids = jnp.arange(levels)
    wet_band = (level_ids[None, None, :] < bottom[:, :, None]).astype(jnp.float32)
    row_start = group_id * sub_rows
    wet_sub = lax.dynamic_slice_in_dim(wet_band, row_start, sub_rows, 0)
    tracer_now = tracers.reshape(num_tracers, sub_rows, columns, levels)
    whole_band = ocean.reshape(3, band_rows, columns, levels)
    current = lax.dynamic_slice_in_dim(whole_band, row_start, sub_rows, 1)
    for step_index in range(STEPS):
        sunlight, heating = optics(tracer_now[2], wet_sub)
        temper = current[2]
        flat_temp = temper.reshape(1, sub_rows, flat_width)
        lower_rim, upper_rim = neighbour_rows(flat_temp, 1, group_id, group_count)
        row_margin = jnp.concatenate(
            [lower_rim.reshape(1, columns, levels), temper, upper_rim.reshape(1, columns, levels)],
            axis=0,
        )
        column_margin = edge_columns(flat_temp, levels).reshape(sub_rows, columns + 2, levels)
        current = ocean_update(current, row_margin, column_margin, heating, wet_sub)
        packed = jnp.concatenate([tracer_now, current[0:2], wet_sub[None]], axis=0)
        field_count = num_tracers + 3
        packed = packed.reshape(field_count, sub_rows, flat_width)
        lower_rim, upper_rim = neighbour_rows(packed, 2, group_id, group_count)
        row_wide = jnp.concatenate([lower_rim, packed, upper_rim], axis=1).reshape(
            field_count, sub_rows + 4, columns, levels
        )
        column_wide = edge_columns(packed, 2 * levels).reshape(
            field_count, sub_rows, columns + 4, levels
        )
        column_change = face_transport(
            column_wide[:num_tracers],
            column_wide[num_tracers : num_tracers + 1],
            column_wide[num_tracers + 2 : num_tracers + 3],
            2,
            columns,
        )
        row_change = face_transport(
            row_wide[:num_tracers],
            row_wide[num_tracers + 1 : num_tracers + 2],
            row_wide[num_tracers + 2 : num_tracers + 3],
            1,
            sub_rows,
        )
        advected = tracer_now - column_change - row_change
        tracer_now = reactions(advected, sunlight, current[2], stoich, wet_sub)
    ocean_final = lax.all_gather(
        current.reshape(3, sub_rows, flat_width), "comp", axis=1, tiled=True
    )
    return (ocean_final, tracer_now.reshape(num_tracers, 1, sub_rows, flat_width))


def solution(mesh):
    in_specs = (P(None, "ty", "tx"), P(None, "ty", "comp", "tx"), P("ty", "tx"), P())
    out_specs = (P(None, "ty", "tx"), P(None, "ty", "comp", "tx"))
    return jax.shard_map(shards, mesh=mesh, in_specs=in_specs, out_specs=out_specs, check_vma=False)
```

profile of v0, /device:TPU:2, one launch (start us, length us, event | category | flops | bytes accessed | tf_op | source)
XLA Modules:
  0.0 92.6 jit_solution(15515678910430724657)
XLA Ops:
  0.7 0.9 %reshape.121 = f32[3,16,4,64]{3,2,1,0:T(4,128)S(1)} reshape(f32[3,16,256]{2,1,0:T(8,128)} %param.4) | data formatting | bytes 98304 | tf_op jit(solution)/shard_map/reshape | solution.py:184
  1.7 1.5 %collective-permute-start.2 = (f32[1,1,256]{2,1,0:T(1,128)S(1)}, f32[1,1,256]{2,1,0:T(1,128)S(1)}, u32[]{:S(2)}, u32[]{:S(2)}) collective-permute-start(f32[1,1,256]{2,1,0:T(1,128)S(1)} %get-tuple-element.68), channel_id=1, source_target_pairs={{0,16},{16,0},{1,17},{17,1},{2,18},{18,2},{3,19},{19,3},{4,20},{20... | collective-permute-start | bytes 3080 | tf_op jit(solution)/shard_map/ppermute | solution.py:43
  3.8 1.9 %collective-permute-start = (f32[1,8,64]{2,1,0:T(8,128)S(1)}, f32[1,8,64]{2,1,0:T(8,128)S(1)}, u32[]{:S(2)}, u32[]{:S(2)}) collective-permute-start(f32[1,8,64]{2,1,0:T(8,128)S(1)} %get-tuple-element.69), channel_id=1, source_target_pairs={{0,1},{1,2},{2,3},{4,5},{5,6},{6,7},{8,9},{9,10},{10,11},{12,13},{... | collective-permute-start | bytes 6152 | tf_op jit(solution)/shard_map/ppermute | solution.py:43
  5.7 3.6 %collective-permute-start.1 = (f32[1,8,64]{2,1,0:T(8,128)S(1)}, f32[1,8,64]{2,1,0:T(8,128)S(1)}, u32[]{:S(2)}, u32[]{:S(2)}) collective-permute-start(f32[1,8,64]{2,1,0:T(8,128)S(1)} %get-tuple-element.70), channel_id=1, source_target_pairs={{1,0},{2,1},{3,2},{5,4},{6,5},{7,6},{9,8},{10,9},{11,10},{13,12},{... | collective-permute-start | bytes 6152 | tf_op jit(solution)/shard_map/ppermute | solution.py:45
  9.6 3.5 %collective-permute-start.4 = (f32[1,1,1,256]{3,2,1,0:T(1,128)S(1)}, f32[1,1,1,256]{3,2,1,0:T(1,128)S(1)}, u32[]{:S(2)}, u32[]{:S(2)}) collective-permute-start(f32[1,1,1,256]{3,2,1,0:T(1,128)S(1)} %fusion.123), channel_id=1, source_target_pairs={{0,4},{4,8},{8,12},{1,5},{5,9},{9,13},{2,6},{6,10},{10,14},{3,7},{... | collective-permute-start | bytes 3080 | tf_op jit(solution)/shard_map/ppermute | solution.py:43
  13.4 1.3 %collective-permute-start.5 = (f32[1,1,1,256]{3,2,1,0:T(1,128)S(1)}, f32[1,1,1,256]{3,2,1,0:T(1,128)S(1)}, u32[]{:S(2)}, u32[]{:S(2)}) collective-permute-start(f32[1,1,1,256]{3,2,1,0:T(1,128)S(1)} %fusion.123), channel_id=1, source_target_pairs={{4,0},{8,4},{12,8},{5,1},{9,5},{13,9},{6,2},{10,6},{14,10},{7,3},{... | collective-permute-start | bytes 3080 | tf_op jit(solution)/shard_map/ppermute | solution.py:45
  14.8 4.1 %collective-permute-done.5 = f32[1,1,1,256]{3,2,1,0:T(1,128)S(1)} collective-permute-done((f32[1,1,1,256]{3,2,1,0:T(1,128)S(1)}, f32[1,1,1,256]{3,2,1,0:T(1,128)S(1)}, u32[]{:S(2)}, u32[]{:S(2)}) %collective-permute-start.5) | collective-permute-done | bytes 1056 | tf_op jit(solution)/shard_map/ppermute | solution.py:45
  19.8 1.5 %collective-permute-start.8 = (f32[1,1,256]{2,1,0:T(1,128)S(1)}, f32[1,1,256]{2,1,0:T(1,128)S(1)}, u32[]{:S(2)}, u32[]{:S(2)}) collective-permute-start(f32[1,1,256]{2,1,0:T(1,128)S(1)} %get-tuple-element.63), channel_id=1, source_target_pairs={{0,16},{16,0},{1,17},{17,1},{2,18},{18,2},{3,19},{19,3},{4,20},{20... | collective-permute-start | bytes 3080 | tf_op jit(solution)/shard_map/ppermute | solution.py:43
  22.0 1.9 %collective-permute-start.6 = (f32[1,8,64]{2,1,0:T(8,128)S(1)}, f32[1,8,64]{2,1,0:T(8,128)S(1)}, u32[]{:S(2)}, u32[]{:S(2)}) collective-permute-start(f32[1,8,64]{2,1,0:T(8,128)S(1)} %get-tuple-element.65), channel_id=1, source_target_pairs={{0,1},{1,2},{2,3},{4,5},{5,6},{6,7},{8,9},{9,10},{10,11},{12,13},{... | collective-permute-start | bytes 6152 | tf_op jit(solution)/shard_map/ppermute | solution.py:43
  23.9 3.6 %collective-permute-start.7 = (f32[1,8,64]{2,1,0:T(8,128)S(1)}, f32[1,8,64]{2,1,0:T(8,128)S(1)}, u32[]{:S(2)}, u32[]{:S(2)}) collective-permute-start(f32[1,8,64]{2,1,0:T(8,128)S(1)} %get-tuple-element.66), channel_id=1, source_target_pairs={{1,0},{2,1},{3,2},{5,4},{6,5},{7,6},{9,8},{10,9},{11,10},{13,12},{... | collective-permute-start | bytes 6152 | tf_op jit(solution)/shard_map/ppermute | solution.py:45
  27.6 3.5 %collective-permute-start.10 = (f32[1,1,1,256]{3,2,1,0:T(1,128)S(1)}, f32[1,1,1,256]{3,2,1,0:T(1,128)S(1)}, u32[]{:S(2)}, u32[]{:S(2)}) collective-permute-start(f32[1,1,1,256]{3,2,1,0:T(1,128)S(1)} %fusion.125), channel_id=1, source_target_pairs={{0,4},{4,8},{8,12},{1,5},{5,9},{9,13},{2,6},{6,10},{10,14},{3,7},{... | collective-permute-start | bytes 3080 | tf_op jit(solution)/shard_map/ppermute | solution.py:43
  31.1 1.3 %collective-permute-start.11 = (f32[1,1,1,256]{3,2,1,0:T(1,128)S(1)}, f32[1,1,1,256]{3,2,1,0:T(1,128)S(1)}, u32[]{:S(2)}, u32[]{:S(2)}) collective-permute-start(f32[1,1,1,256]{3,2,1,0:T(1,128)S(1)} %fusion.125), channel_id=1, source_target_pairs={{4,0},{8,4},{12,8},{5,1},{9,5},{13,9},{6,2},{10,6},{14,10},{7,3},{... | collective-permute-start | bytes 3080 | tf_op jit(solution)/shard_map/ppermute | solution.py:45
  33.1 1.9 %collective-permute-start.12 = (f32[22,8,128]{2,1,0:T(8,128)S(1)}, f32[22,8,128]{2,1,0:T(8,128)S(1)}, u32[]{:S(2)}, u32[]{:S(2)}) collective-permute-start(f32[22,8,128]{2,1,0:T(8,128)S(1)} %get-tuple-element.48), channel_id=1, source_target_pairs={{0,1},{1,2},{2,3},{4,5},{5,6},{6,7},{8,9},{9,10},{10,11},{12,13},{... | collective-permute-start | bytes 270344 | tf_op jit(solution)/shard_map/ppermute | solution.py:43
  35.0 3.6 %collective-permute-start.13 = (f32[22,8,128]{2,1,0:T(8,128)S(1)}, f32[22,8,128]{2,1,0:T(8,128)S(1)}, u32[]{:S(2)}, u32[]{:S(2)}) collective-permute-start(f32[22,8,128]{2,1,0:T(8,128)S(1)} %get-tuple-element.49), channel_id=1, source_target_pairs={{1,0},{2,1},{3,2},{5,4},{6,5},{7,6},{9,8},{10,9},{11,10},{13,12},{... | collective-permute-start | bytes 270344 | tf_op jit(solution)/shard_map/ppermute | solution.py:45
  38.6 1.6 %collective-permute-start.14 = (f32[22,2,256]{2,1,0:T(2,128)S(1)}, f32[22,2,256]{2,1,0:T(2,128)S(1)}, u32[]{:S(2)}, u32[]{:S(2)}) collective-permute-start(f32[22,2,256]{2,1,0:T(2,128)S(1)} %get-tuple-element.50), channel_id=1, source_target_pairs={{0,16},{16,0},{1,17},{17,1},{2,18},{18,2},{3,19},{19,3},{4,20},{20... | collective-permute-start | bytes 135176 | tf_op jit(solution)/shard_map/ppermute | solution.py:43
  42.0 0.8 collective-permute-done.14
  42.8 1.5 %collective-permute-done.15 = f32[22,2,256]{2,1,0:T(2,128)S(1)} collective-permute-done((f32[22,2,256]{2,1,0:T(2,128)S(1)}, f32[22,2,256]{2,1,0:T(2,128)S(1)}, u32[]{:S(2)}, u32[]{:S(2)}) %collective-permute-start.15) | collective-permute-done | bytes 45088 | tf_op jit(solution)/shard_map/ppermute | solution.py:45
  44.3 4.5 %collective-permute-start.16 = (f32[22,1,2,256]{3,2,0,1:T(2,128)S(1)}, f32[22,1,2,256]{3,2,0,1:T(2,128)S(1)}, u32[]{:S(2)}, u32[]{:S(2)}) collective-permute-start(f32[22,1,2,256]{3,2,0,1:T(2,128)S(1)} %select_bitcast_fusion.1), channel_id=1, source_target_pairs={{0,4},{4,8},{8,12},{1,5},{5,9},{9,13},{2,6},{6,10},{10,14},{3,7},{... | collective-permute-start | bytes 135176 | tf_op jit(solution)/shard_map/ppermute | solution.py:43
  49.1 1.3 %collective-permute-start.17 = (f32[22,1,2,256]{3,2,0,1:T(2,128)S(1)}, f32[22,1,2,256]{3,2,0,1:T(2,128)S(1)}, u32[]{:S(2)}, u32[]{:S(2)}) collective-permute-start(f32[22,1,2,256]{3,2,0,1:T(2,128)S(1)} %select_bitcast_fusion.1), channel_id=1, source_target_pairs={{4,0},{8,4},{12,8},{5,1},{9,5},{13,9},{6,2},{10,6},{14,10},{7,3},{... | collective-permute-start | bytes 135176 | tf_op jit(solution)/shard_map/ppermute | solution.py:45
  50.6 4.5 %collective-permute-done.17 = f32[22,1,2,256]{3,2,0,1:T(2,128)S(1)} collective-permute-done((f32[22,1,2,256]{3,2,0,1:T(2,128)S(1)}, f32[22,1,2,256]{3,2,0,1:T(2,128)S(1)}, u32[]{:S(2)}, u32[]{:S(2)}) %collective-permute-start.17) | collective-permute-done | bytes 45088 | tf_op jit(solution)/shard_map/ppermute | solution.py:45
  55.8 0.7 fusion.3
  59.8 1.5 %collective-permute-start.21 = (f32[22,2,256]{2,1,0:T(2,128)S(1)}, f32[22,2,256]{2,1,0:T(2,128)S(1)}, u32[]{:S(2)}, u32[]{:S(2)}) collective-permute-start(f32[22,2,256]{2,1,0:T(2,128)S(1)} %get-tuple-element.47), channel_id=1, source_target_pairs={{16,0},{0,16},{17,1},{1,17},{18,2},{2,18},{19,3},{3,19},{20,4},{4,... | collective-permute-start | bytes 135176 | tf_op jit(solution)/shard_map/ppermute | solution.py:45
  61.3 2.0 %collective-permute-done.20 = f32[22,2,256]{2,1,0:T(2,128)S(1)} collective-permute-done((f32[22,2,256]{2,1,0:T(2,128)S(1)}, f32[22,2,256]{2,1,0:T(2,128)S(1)}, u32[]{:S(2)}, u32[]{:S(2)}) %collective-permute-start.20) | collective-permute-done | bytes 45088 | tf_op jit(solution)/shard_map/ppermute | solution.py:43
  63.9 3.5 %collective-permute-start.22 = (f32[22,1,2,256]{3,2,0,1:T(2,128)S(1)}, f32[22,1,2,256]{3,2,0,1:T(2,128)S(1)}, u32[]{:S(2)}, u32[]{:S(2)}) collective-permute-start(f32[22,1,2,256]{3,2,0,1:T(2,128)S(1)} %select_bitcast_fusion), channel_id=1, source_target_pairs={{0,4},{4,8},{8,12},{1,5},{5,9},{9,13},{2,6},{6,10},{10,14},{3,7},{... | collective-permute-start | bytes 135176 | tf_op jit(solution)/shard_map/ppermute | solution.py:43
  67.4 1.9 %collective-permute-start.18 = (f32[22,8,128]{2,1,0:T(8,128)S(1)}, f32[22,8,128]{2,1,0:T(8,128)S(1)}, u32[]{:S(2)}, u32[]{:S(2)}) collective-permute-start(f32[22,8,128]{2,1,0:T(8,128)S(1)} %get-tuple-element.44), channel_id=1, source_target_pairs={{0,1},{1,2},{2,3},{4,5},{5,6},{6,7},{8,9},{9,10},{10,11},{12,13},{... | collective-permute-start | bytes 270344 | tf_op jit(solution)/shard_map/ppermute | solution.py:43
  69.4 3.6 %collective-permute-start.19 = (f32[22,8,128]{2,1,0:T(8,128)S(1)}, f32[22,8,128]{2,1,0:T(8,128)S(1)}, u32[]{:S(2)}, u32[]{:S(2)}) collective-permute-start(f32[22,8,128]{2,1,0:T(8,128)S(1)} %get-tuple-element.45), channel_id=1, source_target_pairs={{1,0},{2,1},{3,2},{5,4},{6,5},{7,6},{9,8},{10,9},{11,10},{13,12},{... | collective-permute-start | bytes 270344 | tf_op jit(solution)/shard_map/ppermute | solution.py:45
  73.0 1.3 %collective-permute-start.23 = (f32[22,1,2,256]{3,2,0,1:T(2,128)S(1)}, f32[22,1,2,256]{3,2,0,1:T(2,128)S(1)}, u32[]{:S(2)}, u32[]{:S(2)}) collective-permute-start(f32[22,1,2,256]{3,2,0,1:T(2,128)S(1)} %select_bitcast_fusion), channel_id=1, source_target_pairs={{4,0},{8,4},{12,8},{5,1},{9,5},{13,9},{6,2},{10,6},{14,10},{7,3},{... | collective-permute-start | bytes 135176 | tf_op jit(solution)/shard_map/ppermute | solution.py:45
  74.3 4.6 %collective-permute-done.23 = f32[22,1,2,256]{3,2,0,1:T(2,128)S(1)} collective-permute-done((f32[22,1,2,256]{3,2,0,1:T(2,128)S(1)}, f32[22,1,2,256]{3,2,0,1:T(2,128)S(1)}, u32[]{:S(2)}, u32[]{:S(2)}) %collective-permute-start.23) | collective-permute-done | bytes 45088 | tf_op jit(solution)/shard_map/ppermute | solution.py:45
  79.0 0.8 pad_maximum_fusion
  81.3 1.2 %reshape.133 = f32[19,12,4,64]{3,2,1,0:T(4,128)S(1)} reshape(f32[19,12,256]{2,1,0:T(8,128)} %pad_maximum_fusion) | data formatting | bytes 466944 | tf_op jit(solution)/shard_map/slice | solution.py:215
  86.5 0.9 reshape.129
  87.5 4.5 %all_gather.3 = f32[3,16,256]{2,1,0:T(8,128)S(1)} all-gather(f32[3,8,256]{2,1,0:T(8,128)S(1)} %pad_maximum_fusion.15), channel_id=1, replica_groups=mesh['comp'=2,'ty'=4,'tx'=4] {'comp'}, dimensions={1}, use_global_device_ids=true | all-gather | bytes 73728 | tf_op jit(solution)/shard_map/all_gather | solution.py:223
  (171 shorter events, 16.1 us)
Async XLA Ops:
  0.6 8.8 %copy-start = (s32[16,4]{0,1:T(4,128)S(1)}, s32[16,4]{0,1:T(4,128)}, u32[]{:S(2)}) copy-start(s32[16,4]{0,1:T(4,128)} %param.6) | copy-start | bytes 772
  0.6 12.4 %copy-start.1 = (f32[19,1,8,256]{3,2,1,0:T(8,128)S(1)}, f32[19,1,8,256]{3,2,1,0:T(8,128)}, u32[]{:S(2)}) copy-start(f32[19,1,8,256]{3,2,1,0:T(8,128)} %param.5) | copy-start | bytes 466948
  1.7 7.8 %collective-permute-start.2 = (f32[1,1,256]{2,1,0:T(1,128)S(1)}, f32[1,1,256]{2,1,0:T(1,128)S(1)}, u32[]{:S(2)}, u32[]{:S(2)}) collective-permute-start(f32[1,1,256]{2,1,0:T(1,128)S(1)} %get-tuple-element.68), channel_id=1, source_target_pairs={{0,16},{16,0},{1,17},{17,1},{2,18},{18,2},{3,19},{19,3},{4,20},{20... | collective-permute-start | bytes 3080 | tf_op jit(solution)/shard_map/ppermute | solution.py:43
  3.2 6.3 %collective-permute-start.3 = (f32[1,1,256]{2,1,0:T(1,128)S(1)}, f32[1,1,256]{2,1,0:T(1,128)S(1)}, u32[]{:S(2)}, u32[]{:S(2)}) collective-permute-start(f32[1,1,256]{2,1,0:T(1,128)S(1)} %get-tuple-element.67), channel_id=1, source_target_pairs={{16,0},{0,16},{17,1},{1,17},{18,2},{2,18},{19,3},{3,19},{20,4},{4,... | collective-permute-start | bytes 3080 | tf_op jit(solution)/shard_map/ppermute | solution.py:45
  3.8 15.3 %collective-permute-start = (f32[1,8,64]{2,1,0:T(8,128)S(1)}, f32[1,8,64]{2,1,0:T(8,128)S(1)}, u32[]{:S(2)}, u32[]{:S(2)}) collective-permute-start(f32[1,8,64]{2,1,0:T(8,128)S(1)} %get-tuple-element.69), channel_id=1, source_target_pairs={{0,1},{1,2},{2,3},{4,5},{5,6},{6,7},{8,9},{9,10},{10,11},{12,13},{... | collective-permute-start | bytes 6152 | tf_op jit(solution)/shard_map/ppermute | solution.py:43
  5.7 13.3 %collective-permute-start.1 = (f32[1,8,64]{2,1,0:T(8,128)S(1)}, f32[1,8,64]{2,1,0:T(8,128)S(1)}, u32[]{:S(2)}, u32[]{:S(2)}) collective-permute-start(f32[1,8,64]{2,1,0:T(8,128)S(1)} %get-tuple-element.70), channel_id=1, source_target_pairs={{1,0},{2,1},{3,2},{5,4},{6,5},{7,6},{9,8},{10,9},{11,10},{13,12},{... | collective-permute-start | bytes 6152 | tf_op jit(solution)/shard_map/ppermute | solution.py:45
  9.5 39.4 %copy-start.2 = (s32[8,4]{0,1:T(4,128)}, s32[8,4]{0,1:T(4,128)S(1)}, u32[]{:S(2)}) copy-start(s32[8,4]{0,1:T(4,128)S(1)} %constant_dynamic-slice_fusion.3) | copy-start | bytes 388
  9.6 5.2 %collective-permute-start.4 = (f32[1,1,1,256]{3,2,1,0:T(1,128)S(1)}, f32[1,1,1,256]{3,2,1,0:T(1,128)S(1)}, u32[]{:S(2)}, u32[]{:S(2)}) collective-permute-start(f32[1,1,1,256]{3,2,1,0:T(1,128)S(1)} %fusion.123), channel_id=1, source_target_pairs={{0,4},{4,8},{8,12},{1,5},{5,9},{9,13},{2,6},{6,10},{10,14},{3,7},{... | collective-permute-start | bytes 3080 | tf_op jit(solution)/shard_map/ppermute | solution.py:43
  13.4 5.5 %collective-permute-start.5 = (f32[1,1,1,256]{3,2,1,0:T(1,128)S(1)}, f32[1,1,1,256]{3,2,1,0:T(1,128)S(1)}, u32[]{:S(2)}, u32[]{:S(2)}) collective-permute-start(f32[1,1,1,256]{3,2,1,0:T(1,128)S(1)} %fusion.123), channel_id=1, source_target_pairs={{4,0},{8,4},{12,8},{5,1},{9,5},{13,9},{6,2},{10,6},{14,10},{7,3},{... | collective-permute-start | bytes 3080 | tf_op jit(solution)/shard_map/ppermute | solution.py:45
  19.8 7.8 %collective-permute-start.8 = (f32[1,1,256]{2,1,0:T(1,128)S(1)}, f32[1,1,256]{2,1,0:T(1,128)S(1)}, u32[]{:S(2)}, u32[]{:S(2)}) collective-permute-start(f32[1,1,256]{2,1,0:T(1,128)S(1)} %get-tuple-element.63), channel_id=1, source_target_pairs={{0,16},{16,0},{1,17},{17,1},{2,18},{18,2},{3,19},{19,3},{4,20},{20... | collective-permute-start | bytes 3080 | tf_op jit(solution)/shard_map/ppermute | solution.py:43
  21.3 6.3 %collective-permute-start.9 = (f32[1,1,256]{2,1,0:T(1,128)S(1)}, f32[1,1,256]{2,1,0:T(1,128)S(1)}, u32[]{:S(2)}, u32[]{:S(2)}) collective-permute-start(f32[1,1,256]{2,1,0:T(1,128)S(1)} %get-tuple-element.64), channel_id=1, source_target_pairs={{16,0},{0,16},{17,1},{1,17},{18,2},{2,18},{19,3},{3,19},{20,4},{4,... | collective-permute-start | bytes 3080 | tf_op jit(solution)/shard_map/ppermute | solution.py:45
  22.0 10.4 %collective-permute-start.6 = (f32[1,8,64]{2,1,0:T(8,128)S(1)}, f32[1,8,64]{2,1,0:T(8,128)S(1)}, u32[]{:S(2)}, u32[]{:S(2)}) collective-permute-start(f32[1,8,64]{2,1,0:T(8,128)S(1)} %get-tuple-element.65), channel_id=1, source_target_pairs={{0,1},{1,2},{2,3},{4,5},{5,6},{6,7},{8,9},{9,10},{10,11},{12,13},{... | collective-permute-start | bytes 6152 | tf_op jit(solution)/shard_map/ppermute | solution.py:43
  23.9 8.5 %collective-permute-start.7 = (f32[1,8,64]{2,1,0:T(8,128)S(1)}, f32[1,8,64]{2,1,0:T(8,128)S(1)}, u32[]{:S(2)}, u32[]{:S(2)}) collective-permute-start(f32[1,8,64]{2,1,0:T(8,128)S(1)} %get-tuple-element.66), channel_id=1, source_target_pairs={{1,0},{2,1},{3,2},{5,4},{6,5},{7,6},{9,8},{10,9},{11,10},{13,12},{... | collective-permute-start | bytes 6152 | tf_op jit(solution)/shard_map/ppermute | solution.py:45
  27.6 12.6 %collective-permute-start.10 = (f32[1,1,1,256]{3,2,1,0:T(1,128)S(1)}, f32[1,1,1,256]{3,2,1,0:T(1,128)S(1)}, u32[]{:S(2)}, u32[]{:S(2)}) collective-permute-start(f32[1,1,1,256]{3,2,1,0:T(1,128)S(1)} %fusion.125), channel_id=1, source_target_pairs={{0,4},{4,8},{8,12},{1,5},{5,9},{9,13},{2,6},{6,10},{10,14},{3,7},{... | collective-permute-start | bytes 3080 | tf_op jit(solution)/shard_map/ppermute | solution.py:43
  31.1 9.8 %collective-permute-start.11 = (f32[1,1,1,256]{3,2,1,0:T(1,128)S(1)}, f32[1,1,1,256]{3,2,1,0:T(1,128)S(1)}, u32[]{:S(2)}, u32[]{:S(2)}) collective-permute-start(f32[1,1,1,256]{3,2,1,0:T(1,128)S(1)} %fusion.125), channel_id=1, source_target_pairs={{4,0},{8,4},{12,8},{5,1},{9,5},{13,9},{6,2},{10,6},{14,10},{7,3},{... | collective-permute-start | bytes 3080 | tf_op jit(solution)/shard_map/ppermute | solution.py:45
  33.1 23.5 %collective-permute-start.12 = (f32[22,8,128]{2,1,0:T(8,128)S(1)}, f32[22,8,128]{2,1,0:T(8,128)S(1)}, u32[]{:S(2)}, u32[]{:S(2)}) collective-permute-start(f32[22,8,128]{2,1,0:T(8,128)S(1)} %get-tuple-element.48), channel_id=1, source_target_pairs={{0,1},{1,2},{2,3},{4,5},{5,6},{6,7},{8,9},{9,10},{10,11},{12,13},{... | collective-permute-start | bytes 270344 | tf_op jit(solution)/shard_map/ppermute | solution.py:43
  35.0 21.6 %collective-permute-start.13 = (f32[22,8,128]{2,1,0:T(8,128)S(1)}, f32[22,8,128]{2,1,0:T(8,128)S(1)}, u32[]{:S(2)}, u32[]{:S(2)}) collective-permute-start(f32[22,8,128]{2,1,0:T(8,128)S(1)} %get-tuple-element.49), channel_id=1, source_target_pairs={{1,0},{2,1},{3,2},{5,4},{6,5},{7,6},{9,8},{10,9},{11,10},{13,12},{... | collective-permute-start | bytes 270344 | tf_op jit(solution)/shard_map/ppermute | solution.py:45
  38.6 4.1 %collective-permute-start.14 = (f32[22,2,256]{2,1,0:T(2,128)S(1)}, f32[22,2,256]{2,1,0:T(2,128)S(1)}, u32[]{:S(2)}, u32[]{:S(2)}) collective-permute-start(f32[22,2,256]{2,1,0:T(2,128)S(1)} %get-tuple-element.50), channel_id=1, source_target_pairs={{0,16},{16,0},{1,17},{17,1},{2,18},{18,2},{3,19},{19,3},{4,20},{20... | collective-permute-start | bytes 135176 | tf_op jit(solution)/shard_map/ppermute | solution.py:43
  40.2 4.0 %collective-permute-start.15 = (f32[22,2,256]{2,1,0:T(2,128)S(1)}, f32[22,2,256]{2,1,0:T(2,128)S(1)}, u32[]{:S(2)}, u32[]{:S(2)}) collective-permute-start(f32[22,2,256]{2,1,0:T(2,128)S(1)} %get-tuple-element.51), channel_id=1, source_target_pairs={{16,0},{0,16},{17,1},{1,17},{18,2},{2,18},{19,3},{3,19},{20,4},{4,... | collective-permute-start | bytes 135176 | tf_op jit(solution)/shard_map/ppermute | solution.py:45
  44.3 6.2 %collective-permute-start.16 = (f32[22,1,2,256]{3,2,0,1:T(2,128)S(1)}, f32[22,1,2,256]{3,2,0,1:T(2,128)S(1)}, u32[]{:S(2)}, u32[]{:S(2)}) collective-permute-start(f32[22,1,2,256]{3,2,0,1:T(2,128)S(1)} %select_bitcast_fusion.1), channel_id=1, source_target_pairs={{0,4},{4,8},{8,12},{1,5},{5,9},{9,13},{2,6},{6,10},{10,14},{3,7},{... | collective-permute-start | bytes 135176 | tf_op jit(solution)/shard_map/ppermute | solution.py:43
  49.1 5.9 %collective-permute-start.17 = (f32[22,1,2,256]{3,2,0,1:T(2,128)S(1)}, f32[22,1,2,256]{3,2,0,1:T(2,128)S(1)}, u32[]{:S(2)}, u32[]{:S(2)}) collective-permute-start(f32[22,1,2,256]{3,2,0,1:T(2,128)S(1)} %select_bitcast_fusion.1), channel_id=1, source_target_pairs={{4,0},{8,4},{12,8},{5,1},{9,5},{13,9},{6,2},{10,6},{14,10},{7,3},{... | collective-permute-start | bytes 135176 | tf_op jit(solution)/shard_map/ppermute | solution.py:45
  58.0 0.7 copy-start.5
  59.3 4.1 %collective-permute-start.20 = (f32[22,2,256]{2,1,0:T(2,128)S(1)}, f32[22,2,256]{2,1,0:T(2,128)S(1)}, u32[]{:S(2)}, u32[]{:S(2)}) collective-permute-start(f32[22,2,256]{2,1,0:T(2,128)S(1)} %get-tuple-element.46), channel_id=1, source_target_pairs={{0,16},{16,0},{1,17},{17,1},{2,18},{18,2},{3,19},{19,3},{4,20},{20... | collective-permute-start | bytes 135176 | tf_op jit(solution)/shard_map/ppermute | solution.py:43
  59.8 4.0 %collective-permute-start.21 = (f32[22,2,256]{2,1,0:T(2,128)S(1)}, f32[22,2,256]{2,1,0:T(2,128)S(1)}, u32[]{:S(2)}, u32[]{:S(2)}) collective-permute-start(f32[22,2,256]{2,1,0:T(2,128)S(1)} %get-tuple-element.47), channel_id=1, source_target_pairs={{16,0},{0,16},{17,1},{1,17},{18,2},{2,18},{19,3},{3,19},{20,4},{4,... | collective-permute-start | bytes 135176 | tf_op jit(solution)/shard_map/ppermute | solution.py:45
  63.9 10.4 %collective-permute-start.22 = (f32[22,1,2,256]{3,2,0,1:T(2,128)S(1)}, f32[22,1,2,256]{3,2,0,1:T(2,128)S(1)}, u32[]{:S(2)}, u32[]{:S(2)}) collective-permute-start(f32[22,1,2,256]{3,2,0,1:T(2,128)S(1)} %select_bitcast_fusion), channel_id=1, source_target_pairs={{0,4},{4,8},{8,12},{1,5},{5,9},{9,13},{2,6},{6,10},{10,14},{3,7},{... | collective-permute-start | bytes 135176 | tf_op jit(solution)/shard_map/ppermute | solution.py:43
  67.4 12.3 %collective-permute-start.18 = (f32[22,8,128]{2,1,0:T(8,128)S(1)}, f32[22,8,128]{2,1,0:T(8,128)S(1)}, u32[]{:S(2)}, u32[]{:S(2)}) collective-permute-start(f32[22,8,128]{2,1,0:T(8,128)S(1)} %get-tuple-element.44), channel_id=1, source_target_pairs={{0,1},{1,2},{2,3},{4,5},{5,6},{6,7},{8,9},{9,10},{10,11},{12,13},{... | collective-permute-start | bytes 270344 | tf_op jit(solution)/shard_map/ppermute | solution.py:43
  69.4 10.4 %collective-permute-start.19 = (f32[22,8,128]{2,1,0:T(8,128)S(1)}, f32[22,8,128]{2,1,0:T(8,128)S(1)}, u32[]{:S(2)}, u32[]{:S(2)}) collective-permute-start(f32[22,8,128]{2,1,0:T(8,128)S(1)} %get-tuple-element.45), channel_id=1, source_target_pairs={{1,0},{2,1},{3,2},{5,4},{6,5},{7,6},{9,8},{10,9},{11,10},{13,12},{... | collective-permute-start | bytes 270344 | tf_op jit(solution)/shard_map/ppermute | solution.py:45
  73.0 5.9 %collective-permute-start.23 = (f32[22,1,2,256]{3,2,0,1:T(2,128)S(1)}, f32[22,1,2,256]{3,2,0,1:T(2,128)S(1)}, u32[]{:S(2)}, u32[]{:S(2)}) collective-permute-start(f32[22,1,2,256]{3,2,0,1:T(2,128)S(1)} %select_bitcast_fusion), channel_id=1, source_target_pairs={{4,0},{8,4},{12,8},{5,1},{9,5},{13,9},{6,2},{10,6},{14,10},{7,3},{... | collective-permute-start | bytes 135176 | tf_op jit(solution)/shard_map/ppermute | solution.py:45
  82.7 0.7 copy-start.4
  84.6 0.7 copy-start.3
  84.6 0.7 copy-start.8
  84.6 0.7 copy-start.10
  (3 other events, 1.8 us)
where the time goes:
time: 93.3 us; the launch traced here: 92.6 us
  starting transfers between devices  50.6 us (54%)
  waiting for transfers between devices  18.2 us (20%)
  local copies, waits for them, and re-layouts  11.4 us (12%)
  other arithmetic  5.36 us (6%)
  blocking collectives  4.49 us (5%)
  between operations  1.49 us (2%)
  matrix products  1.02 us (1%)
    ppermute x12, starting transfers between devices, extended_2(): lax.ppermute(tail, axis, [(i, (i + 1) % count) for i in range(ends)])  27.9 us
    ppermute x12, starting transfers between devices, extended_2(): lax.ppermute(head, axis, [((i + 1) % count, i) for i in range(ends)])  22.8 us
    ppermute x12, waiting for transfers between devices, extended_2(): lax.ppermute(head, axis, [((i + 1) % count, i) for i in range(ends)])  15.2 us
    all_gather x1, blocking collectives, shards(): lax.all_gather(current.reshape(3, sub_rows, flat_width), 'comp', axis=1,...  4.49 us
    unnamed x27, local copies, waits for them, and re-layouts  4.1 us
    ppermute x12, waiting for transfers between devices, extended_2(): lax.ppermute(tail, axis, [(i, (i + 1) % count) for i in range(ends)])  2.93 us
    mul x8, other arithmetic, face_transport(): flux = ADVECT * speed * jnp.where(speed > 0.0, from_left, from_right)  2.52 us
  transfers between devices with their start and end apart: 24, of which 8 were waited for; matrix products, arithmetic and copies ran while one was open for 5% of the time, Pallas kernels for 0%

commit v1 on v0

v1 whole, which is shorter than its diff:
```python
import functools

import jax
import jax.numpy as jnp
from jax import lax
from jax.experimental import pallas as pl
from jax.experimental.pallas import tpu as pltpu
from jax.sharding import PartitionSpec as P

LEV = 64
STEPS = 2

ATTEN_WATER = 0.04
ATTEN_CHL = 0.03
PRESSURE = 0.05
TIME_STEP = 0.2
CORIOLIS = 1.0
DAMPING = 0.05
HEAT_GAIN = 2.0
DIFFUSE = 0.2
ADVECT = 0.08
GROWTH = 1.0
HALF_LIGHT = 0.2
HALF_NUTRIENT = 0.5
TEMP_COEF = 0.1
GRAZE = 0.8
HALF_PREY = 0.3
MORTAL = 0.1
REMIN = 0.2
CHL_RELAX = 0.3
CHL_RATIO = 0.5
CHL_GAIN = 0.2
ASSIM = 0.3
GRAZER_LOSS = 0.05
REACT_STEP = 0.2

MESH = pl.DeviceIdType.MESH
HALF = 2 * LEV
CORE = 5
CHUNK = 7
F32 = jnp.float32


def kernel(
    ncomp, nty, ntx,
    tr_in, oc_in, bottom, stoich,
    tr_out, oc_out,
    q0, q1, s0, s1, s2, band,
    rim_q, west_q, east_q, rim_s, west_s, east_s,
    load_sem, send_sem, recv_sem, gsend_sem, grecv_sem,
):
    comp = lax.axis_index("comp")
    ty = lax.axis_index("ty")
    tx = lax.axis_index("tx")
    tile = ty * ncomp + comp
    rows = q0.shape[1]
    ntr = q0.shape[0]
    start = pl.multiple_of(comp * rows, rows)

    load_o = pltpu.make_async_copy(oc_in.at[:, pl.ds(start, rows), :], s0.at[0:3], load_sem.at[0])
    load_q = pltpu.make_async_copy(tr_in.at[:, 0], q0, load_sem.at[1])
    load_o.start()
    load_q.start()

    up = jnp.maximum(tile - 1, 0)
    down = jnp.minimum(tile + 1, ncomp * nty - 1)
    targets = (
        {"comp": lax.rem(down, ncomp), "ty": lax.div(down, ncomp)},
        {"comp": lax.rem(up, ncomp), "ty": lax.div(up, ncomp)},
        {"tx": jnp.minimum(tx + 1, ntx - 1)},
        {"tx": jnp.maximum(tx - 1, 0)},
    )
    has_down, has_up = tile < ncomp * nty - 1, tile > 0
    has_east, has_west = tx < ntx - 1, tx > 0
    sends = (has_down, has_up, has_east, has_west)
    gets = (has_up, has_down, has_west, has_east)

    for ref in (rim_q, west_q, east_q, rim_s, west_s, east_s):
        ref[...] = jnp.zeros(ref.shape, F32)

    barrier = pltpu.get_barrier_semaphore()
    for way in range(4):
        @pl.when(sends[way])
        def _(way=way):
            pl.semaphore_signal(barrier, inc=1, device_id=targets[way], device_id_type=MESH)
    for hop in range(1, ncomp):
        pl.semaphore_signal(
            barrier, inc=1, device_id={"comp": lax.rem(comp + hop, ncomp)}, device_id_type=MESH
        )

    lane = lax.broadcasted_iota(jnp.int32, (rows, HALF), 1)
    sub = lax.broadcasted_iota(jnp.int32, (rows, HALF), 0)
    low = lane < LEV
    level = lax.rem(lane, LEV)
    floor = bottom[pl.ds(start, rows), :]
    wet = [
        (level < jnp.where(low, floor[:, 2 * i : 2 * i + 1], floor[:, 2 * i + 1 : 2 * i + 2])).astype(F32)
        for i in range(2)
    ]
    for i in range(2):
        s0[3, :, i * HALF : (i + 1) * HALF] = wet[i]

    a = lax.broadcasted_iota(jnp.int32, (HALF, HALF), 0)
    b = lax.broadcasted_iota(jnp.int32, (HALF, HALF), 1)
    same = (a < LEV) == (b < LEV)
    incl = jnp.where(same & (a <= b), 1.0, 0.0).astype(jnp.bfloat16)
    excl = jnp.where(same & (a < b), 1.0, 0.0).astype(jnp.bfloat16)

    expect = sum(jnp.where(flag, 1, 0) for flag in sends) + (ncomp - 1)
    pl.semaphore_wait(barrier, expect)

    def exchange(step, kind, state, rim, west, east, count):
        ends = (
            (state.at[0:count, rows - 2 : rows, :], rim.at[step, 0:count, rows - 2 : rows, :]),
            (state.at[0:count, 0:2, :], rim.at[step, 0:count, 0:2, :]),
            (state.at[0:count, :, HALF : 2 * HALF], west.at[step, 0:count]),
            (state.at[0:count, :, 0:HALF], east.at[step, 0:count]),
        )
        return [
            pltpu.make_async_remote_copy(
                src_ref=source,
                dst_ref=target,
                send_sem=send_sem.at[step, kind, way],
                recv_sem=recv_sem.at[step, kind, way],
                device_id=targets[way],
                device_id_type=MESH,
            )
            for way, (source, target) in enumerate(ends)
        ]

    def begin(copies):
        for way in range(4):
            @pl.when(sends[way])
            def _(way=way):
                copies[way].start()

    def arrive(copies):
        for way in range(4):
            @pl.when(gets[way])
            def _(way=way):
                copies[way].wait_recv()

    def left(copies):
        for way in range(4):
            @pl.when(sends[way])
            def _(way=way):
                copies[way].wait_send()

    def level_sums(parts, ladder):
        x = jnp.concatenate(parts, axis=0)
        high = x.astype(jnp.bfloat16)
        rest = x - high.astype(F32)
        mid = rest.astype(jnp.bfloat16)
        last = (rest - mid.astype(F32)).astype(jnp.bfloat16)
        n = x.shape[0]
        y = jnp.dot(
            jnp.concatenate([high, mid, last], axis=0), ladder, preferred_element_type=F32
        )
        y = y[0:n] + y[n : 2 * n] + y[2 * n : 3 * n]
        return [y[i * rows : (i + 1) * rows] for i in range(len(parts))]

    def pick(mask, x, y):
        if x.ndim == 3:
            mask = jnp.broadcast_to(mask[None], x.shape)
        return jnp.where(mask, x, y)

    def swap(x):
        return pltpu.roll(x, LEV, axis=x.ndim - 1)

    def spin(x, shift):
        return pltpu.roll(x, shift, axis=x.ndim - 2)

    first, first_two, final = sub < 1, sub < 2, sub > rows - 2

    def next_row(x, rim):
        return spin(pick(first, rim, x), rows - 1)

    def after_row(x, rim):
        return spin(pick(first_two, rim, x), rows - 2)

    def prev_row(x, rim):
        return spin(pick(final, rim, x), 1)

    def limited(below, middle, above, pos, sign_half, speed, q_a, q_b):
        other = pick(pos, below, above)
        least = jnp.minimum(other, middle)
        most = jnp.maximum(other, middle)
        slope = jnp.maximum(least, 0.0) + jnp.minimum(most, 0.0)
        return speed * (pick(pos, q_a, q_b) + sign_half * slope)

    def halves(ref, *lead):
        return [ref[(*lead, slice(None), slice(0, HALF))], ref[(*lead, slice(None), slice(HALF, 2 * HALF))]]

    copies_s = exchange(0, 0, s0, rim_s, west_s, east_s, 4)
    copies_q = exchange(0, 1, q0, rim_q, west_q, east_q, ntr)
    load_o.wait()
    begin(copies_s)
    load_q.wait()
    begin(copies_q)
    pending = copies_s + copies_q
    pend_s, pend_q = [copies_s], [copies_q]

    states = (s0, s1, s2)
    gathers = []
    wet_ring = None
    for step in range(STEPS):
        q_ref, state, after = (q0, q1)[step], states[step], states[step + 1]
        u, v, temp = (halves(state, k) for k in range(3))
        absorb = [
            (ATTEN_WATER + ATTEN_CHL * jnp.maximum(c, 0.0)) * w
            for c, w in zip(halves(q_ref, 2), wet)
        ]
        above = level_sums(absorb, excl)
        sunlight = [jnp.exp(-x) for x in above]
        heating = [s * (1.0 - jnp.exp(-x)) * w for s, x, w in zip(sunlight, absorb, wet)]

        arrive(copies_s)
        if step == 0:
            wet_line = [west_s[0, 3], *wet, east_s[0, 3]]
            wet_rim = halves(rim_s, 0, 3)
            turned = [swap(x) for x in wet_line]
            col_gate = [
                wet_line[i] * pick(low, turned[i], turned[i + 1]) for i in range(3)
            ]
            row_gate = [w * next_row(w, r) for w, r in zip(wet, wet_rim)]
            rim_gate = [r * spin(w, rows - 1) for w, r in zip(wet, wet_rim)]
        line = [west_s[step, 2], *temp, east_s[step, 2]]
        rim = halves(rim_s, step, 2)
        sums = level_sums(line + rim, incl)
        press, press_rim = sums[:4], sums[4:]
        turned = [swap(x) for x in press]
        u_line = [west_s[step, 0], *u, east_s[step, 0]]
        v_line = [west_s[step, 1], *v, east_s[step, 1]]
        new_u = []
        for i in range(4):
            east = pick(low, turned[i], turned[min(i + 1, 3)])
            west = pick(low, turned[max(i - 1, 0)], turned[i])
            slope = (0.5 * PRESSURE) * (east - west)
            new_u.append(
                wet_line[i] * ((1.0 - DAMPING) * u_line[i] + TIME_STEP * (CORIOLIS * v_line[i] - slope))
            )
        u_rim, v_rim = halves(rim_s, step, 0), halves(rim_s, step, 1)
        new_v, new_v_rim, new_temp = [], [], []
        turned = [swap(x) for x in line]
        for i in range(2):
            slope = (0.5 * PRESSURE) * (
                next_row(press[i + 1], press_rim[i]) - prev_row(press[i + 1], press_rim[i])
            )
            new_v.append(
                wet[i] * ((1.0 - DAMPING) * v[i] - TIME_STEP * (CORIOLIS * u[i] + slope))
            )
            slope = (0.5 * PRESSURE) * (
                next_row(press_rim[i], press[i + 1]) - prev_row(press_rim[i], press[i + 1])
            )
            new_v_rim.append(
                wet_rim[i] * ((1.0 - DAMPING) * v_rim[i] - TIME_STEP * (CORIOLIS * u_rim[i] + slope))
            )
            spread = (
                next_row(temp[i], rim[i])
                + prev_row(temp[i], rim[i])
                + pick(low, turned[i + 1], turned[i + 2])
                + pick(low, turned[i], turned[i + 1])
                - 4.0 * temp[i]
            )
            new_temp.append(
                wet[i] * (temp[i] + TIME_STEP * (HEAT_GAIN * heating[i] + DIFFUSE * spread))
            )
        for i in range(2):
            cols = slice(i * HALF, (i + 1) * HALF)
            after[0, :, cols] = new_u[i + 1]
            after[1, :, cols] = new_v[i]
            after[2, :, cols] = new_temp[i]
        if step + 1 < STEPS:
            copies_s = exchange(step + 1, 0, after, rim_s, west_s, east_s, 3)
            begin(copies_s)
            pend_s.append(copies_s)
        else:
            for hop in range(1, ncomp):
                copy = pltpu.make_async_remote_copy(
                    src_ref=after,
                    dst_ref=band.at[:, pl.ds(start, rows), :],
                    send_sem=gsend_sem.at[hop - 1],
                    recv_sem=grecv_sem.at[hop - 1],
                    device_id={"comp": lax.rem(comp + hop, ncomp)},
                    device_id_type=MESH,
                )
                copy.start()
                gathers.append(copy)
            band[:, pl.ds(start, rows), :] = after[...]

        turned = [swap(x) for x in new_u]
        col_speed = [
            (0.5 * ADVECT) * (new_u[i] + pick(low, turned[i], turned[i + 1])) * col_gate[i]
            for i in range(3)
        ]
        row_speed = [
            (0.5 * ADVECT) * (new_v[i] + next_row(new_v[i], new_v_rim[i])) * row_gate[i]
            for i in range(2)
        ]
        rim_speed = [
            (0.5 * ADVECT) * (new_v_rim[i] + spin(new_v[i], rows - 1)) * rim_gate[i]
            for i in range(2)
        ]

        def gauge(speeds):
            return [(x > 0.0, jnp.where(x > 0.0, 0.5, -0.5), x) for x in speeds]

        col_gauge, row_gauge, rim_gauge = gauge(col_speed), gauge(row_speed), gauge(rim_speed)

        arrive(copies_q)

        def advect(lo, hi):
            part = slice(lo, hi)
            q = [q_ref[part, :, 0:HALF], q_ref[part, :, HALF : 2 * HALF]]
            line = [west_q[step, part], *q, east_q[step, part]]
            rim = [rim_q[step, part, :, 0:HALF], rim_q[step, part, :, HALF : 2 * HALF]]
            turned = [swap(x) for x in line]
            flux = []
            for i in range(3):
                east = pick(low, turned[i], turned[i + 1])
                west = pick(low, turned[max(i - 1, 0)], turned[i])
                here = line[i]
                pos, sign_half, speed = col_gauge[i]
                flux.append(
                    limited(
                        here - west, east - here, line[i + 1] - east,
                        pos, sign_half, speed, here, east,
                    )
                )
            turned = [swap(x) for x in flux]
            out = []
            for i in range(2):
                value = q[i] - (flux[i + 1] - pick(low, turned[i], turned[i + 1]))
                after_one = next_row(q[i], rim[i])
                pos, sign_half, speed = row_gauge[i]
                inner = limited(
                    q[i] - prev_row(q[i], rim[i]), after_one - q[i], after_row(q[i], rim[i]) - after_one,
                    pos, sign_half, speed, q[i], after_one,
                )
                after_one = spin(q[i], rows - 1)
                pos, sign_half, speed = rim_gauge[i]
                outer = limited(
                    rim[i] - spin(rim[i], 1), after_one - rim[i], spin(q[i], rows - 2) - after_one,
                    pos, sign_half, speed, rim[i], after_one,
                )
                out.append(value - (inner - prev_row(inner, outer)))
            return out

        def put(lo, hi, i, value):
            cols = slice(i * HALF, (i + 1) * HALF)
            if step + 1 < STEPS:
                q1[lo:hi, :, cols] = value
            else:
                tr_out[lo:hi, 0, :, cols] = value

        core = advect(0, CORE)
        net = []
        for i in range(2):
            adv = [core[i][k] for k in range(CORE)]
            nutrient, phyto, chloro, grazer, detritus = (jnp.maximum(x, 0.0) for x in adv)
            uptake = (
                GROWTH
                * sunlight[i]
                / (sunlight[i] + HALF_LIGHT)
                * nutrient
                / (nutrient + HALF_NUTRIENT)
                * jnp.exp(TEMP_COEF * new_temp[i])
            )
            growth = uptake * phyto
            grazing = GRAZE * grazer * phyto * phyto / (phyto * phyto + HALF_PREY)
            dying = MORTAL * phyto
            remineral = REMIN * detritus
            changes = (
                remineral - growth,
                growth - grazing - dying,
                CHL_RELAX * (CHL_RATIO * phyto - chloro) + CHL_GAIN * growth,
                ASSIM * grazing - GRAZER_LOSS * grazer,
                dying + (1.0 - ASSIM) * grazing + GRAZER_LOSS * grazer - remineral,
            )
            for k in range(CORE):
                put(k, k + 1, i, ((adv[k] + REACT_STEP * changes[k]) * wet[i])[None])
            net.append(REACT_STEP * (growth - remineral))
        for lo in range(CORE, ntr, CHUNK):
            hi = min(lo + CHUNK, ntr)
            adv = advect(lo, hi)
            for i in range(2):
                for k in range(lo, hi):
                    put(k, k + 1, i, ((adv[i][k - lo] + stoich[k - CORE] * net[i]) * wet[i])[None])
        if step + 1 < STEPS:
            copies_q = exchange(step + 1, 1, q1, rim_q, west_q, east_q, ntr)
            begin(copies_q)
            pend_q.append(copies_q)

    for copies in pend_s + pend_q:
        left(copies)
    for copy in gathers:
        copy.wait()
    oc_out[...] = band[...]


def shards(ocean, tracers, bottom, stoich):
    ncomp, nty, ntx = (lax.axis_size(name) for name in ("comp", "ty", "tx"))
    ntr, _, rows, width = tracers.shape
    vmem = pl.BlockSpec(memory_space=pltpu.VMEM)
    tr_out, oc_out = pl.pallas_call(
        functools.partial(kernel, ncomp, nty, ntx),
        out_shape=(
            jax.ShapeDtypeStruct(tracers.shape, F32),
            jax.ShapeDtypeStruct(ocean.shape, F32),
        ),
        in_specs=[
            pl.BlockSpec(memory_space=pl.ANY),
            pl.BlockSpec(memory_space=pl.ANY),
            vmem,
            pl.BlockSpec(memory_space=pltpu.SMEM),
        ],
        out_specs=(vmem, vmem),
        scratch_shapes=[
            pltpu.VMEM((ntr, rows, width), F32),
            pltpu.VMEM((ntr, rows, width), F32),
            pltpu.VMEM((4, rows, width), F32),
            pltpu.VMEM((3, rows, width), F32),
            pltpu.VMEM((3, rows, width), F32),
            pltpu.VMEM(ocean.shape, F32),
            pltpu.VMEM((STEPS, ntr, rows, width), F32),
            pltpu.VMEM((STEPS, ntr, rows, HALF), F32),
            pltpu.VMEM((STEPS, ntr, rows, HALF), F32),
            pltpu.VMEM((STEPS, 4, rows, width), F32),
            pltpu.VMEM((STEPS, 4, rows, HALF), F32),
            pltpu.VMEM((STEPS, 4, rows, HALF), F32),
            pltpu.SemaphoreType.DMA((2,)),
            pltpu.SemaphoreType.DMA((STEPS, 2, 4)),
            pltpu.SemaphoreType.DMA((STEPS, 2, 4)),
            pltpu.SemaphoreType.DMA((max(ncomp - 1, 1),)),
            pltpu.SemaphoreType.DMA((max(ncomp - 1, 1),)),
        ],
        compiler_params=pltpu.CompilerParams(
            collective_id=0, has_side_effects=True, vmem_limit_bytes=32 * 1024 * 1024
        ),
    )(tracers, ocean, bottom, stoich)
    return oc_out, tr_out


def solution(mesh):
    in_specs = (P(None, "ty", "tx"), P(None, "ty", "comp", "tx"), P("ty", "tx"), P())
    out_specs = (P(None, "ty", "tx"), P(None, "ty", "comp", "tx"))
    return jax.shard_map(shards, mesh=mesh, in_specs=in_specs, out_specs=out_specs, check_vma=False)
```

time: 93.3 us -> 19.3 us (0.21)
  the two profiles are of different devices: /device:TPU:2 before, /device:TPU:0 now
where the time goes in v1:
time: 19.3 us; the launch traced here: 19.1 us
  Pallas kernels  14.7 us (76%)
  local copies, waits for them, and re-layouts  3.76 us (19%)
  between operations  0.65 us (3%)
    pallas_call x1, Pallas kernels, shards(): pl.pallas_call(functools.partial(kernel, ncomp, nty, ntx), out_shape=(jax...  14.7 us
    unnamed x9, local copies, waits for them, and re-layouts  3.76 us

profile of v1, /device:TPU:0, one launch (start us, length us, event | category | flops | bytes accessed | tf_op | source)
XLA Modules:
  0.0 19.1 jit_solution(4439166518344430972)
XLA Ops:
  0.6 0.0 copy-start.2
  0.6 0.8 %copy.6.bottom = s32[16,4]{1,0:T(8,128)S(1)} copy(s32[16,4]{0,1:T(4,128)} %param.6) | data formatting | bytes 512 | tf_op args[2]
  1.4 0.0 copy-done.2
  1.4 0.0 copy-start
  1.4 0.9 %copy-done = f32[19,1,8,256]{3,2,1,0:T(8,128)S(1)} copy-done((f32[19,1,8,256]{3,2,1,0:T(8,128)S(1)}, f32[19,1,8,256]{3,2,1,0:T(8,128)}, u32[]{:S(2)}) %copy-start) | copy-done | bytes 155672
  2.3 0.0 copy-start.1
  2.3 0.8 %copy-done.1 = f32[3,16,256]{2,1,0:T(8,128)S(1)} copy-done((f32[3,16,256]{2,1,0:T(8,128)S(1)}, f32[3,16,256]{2,1,0:T(8,128)}, u32[]{:S(2)}) %copy-start.1) | copy-done | bytes 49176
  3.1 14.7 %shard_map.59 = (f32[19,1,8,256]{3,2,1,0:T(8,128)S(1)}, f32[3,16,256]{2,1,0:T(8,128)S(1)}) custom-call(f32[19,1,8,256]{3,2,1,0:T(8,128)S(1)} %copy-done, f32[3,16,256]{2,1,0:T(8,128)S(1)} %copy-done.1, s32[16,4]{1,0:T(8,128)S(1)} %copy.6.bottom, f32[14]{0:T(128)S(1)} %copy-done.2), custom_call_target="tpu_custom_call" | custom-call | tf_op jit(solution)/shard_map/pallas_call | solution.py:405
  17.8 0.6 %copy.9 = f32[3,16,256]{2,1,0:T(8,128)} copy(f32[3,16,256]{2,1,0:T(8,128)S(1)} %get-tuple-element.8) | data formatting | bytes 98304
  18.4 0.7 %copy.10 = f32[19,1,8,256]{3,2,1,0:T(8,128)} copy(f32[19,1,8,256]{3,2,1,0:T(8,128)S(1)} %get-tuple-element.9) | data formatting | bytes 311296
Async XLA Ops:
  0.6 0.8 %copy-start.2 = (f32[14]{0:T(128)S(1)}, f32[14]{0:T(128)}, u32[]{:S(2)}) copy-start(f32[14]{0:T(128)} %stoich.1) | copy-start | bytes 172
  1.4 0.9 %copy-start = (f32[19,1,8,256]{3,2,1,0:T(8,128)S(1)}, f32[19,1,8,256]{3,2,1,0:T(8,128)}, u32[]{:S(2)}) copy-start(f32[19,1,8,256]{3,2,1,0:T(8,128)} %tr_in.1) | copy-start | bytes 466948
  2.3 0.8 %copy-start.1 = (f32[3,16,256]{2,1,0:T(8,128)S(1)}, f32[3,16,256]{2,1,0:T(8,128)}, u32[]{:S(2)}) copy-start(f32[3,16,256]{2,1,0:T(8,128)} %oc_in.1) | copy-start | bytes 147460

commit v2 on v1

--- a/solution.py
+++ b/solution.py
@@ -43,9 +43,9 @@
 
 def kernel(
     ncomp, nty, ntx,
-    tr_in, oc_in, bottom, stoich,
+    tr_in, oc_in, bottom_in, stoich_in,
     tr_out, oc_out,
-    q0, q1, s0, s1, s2, band,
+    bottom, stoich, floors, q0, q1, s0, s1, chl, u_all, v_all, wet_all, sun_all,
     rim_q, west_q, east_q, rim_s, west_s, east_s,
     load_sem, send_sem, recv_sem, gsend_sem, grecv_sem,
 ):
@@ -55,12 +55,16 @@
     tile = ty * ncomp + comp
     rows = q0.shape[1]
     ntr = q0.shape[0]
+    band = s0.shape[1]
     start = pl.multiple_of(comp * rows, rows)
-
-    load_o = pltpu.make_async_copy(oc_in.at[:, pl.ds(start, rows), :], s0.at[0:3], load_sem.at[0])
+    mine = pl.ds(start, rows)
+
+    load_o = pltpu.make_async_copy(oc_in, s0.at[0:3], load_sem.at[0])
     load_q = pltpu.make_async_copy(tr_in.at[:, 0], q0, load_sem.at[1])
-    load_o.start()
-    load_q.start()
+    load_b = pltpu.make_async_copy(bottom_in, bottom, load_sem.at[2])
+    load_c = pltpu.make_async_copy(stoich_in, stoich, load_sem.at[3])
+    for load in (load_b, load_o, load_q, load_c):
+        load.start()
 
     up = jnp.maximum(tile - 1, 0)
     down = jnp.minimum(tile + 1, ncomp * nty - 1)
@@ -70,10 +74,20 @@
         {"tx": jnp.minimum(tx + 1, ntx - 1)},
         {"tx": jnp.maximum(tx - 1, 0)},
     )
+    ocean_targets = (
+        {"ty": jnp.minimum(ty + 1, nty - 1)},
+        {"ty": jnp.maximum(ty - 1, 0)},
+        targets[2],
+        targets[3],
+    )
+    peers = [{"comp": lax.rem(comp + hop, ncomp)} for hop in range(1, ncomp)]
     has_down, has_up = tile < ncomp * nty - 1, tile > 0
     has_east, has_west = tx < ntx - 1, tx > 0
     sends = (has_down, has_up, has_east, has_west)
     gets = (has_up, has_down, has_west, has_east)
+    has_next, has_last = ty < nty - 1, ty > 0
+    ocean_sends = (has_next, has_last, has_east, has_west)
+    ocean_gets = (has_last, has_next, has_west, has_east)
 
     for ref in (rim_q, west_q, east_q, rim_s, west_s, east_s):
         ref[...] = jnp.zeros(ref.shape, F32)
@@ -83,21 +97,36 @@
         @pl.when(sends[way])
         def _(way=way):
             pl.semaphore_signal(barrier, inc=1, device_id=targets[way], device_id_type=MESH)
-    for hop in range(1, ncomp):
-        pl.semaphore_signal(
-            barrier, inc=1, device_id={"comp": lax.rem(comp + hop, ncomp)}, device_id_type=MESH
-        )
+    for way in range(2):
+        @pl.when(ocean_sends[way])
+        def _(way=way):
+            pl.semaphore_signal(barrier, inc=1, device_id=ocean_targets[way], device_id_type=MESH)
+    for peer in peers:
+        pl.semaphore_signal(barrier, inc=1, device_id=peer, device_id_type=MESH)
 
     lane = lax.broadcasted_iota(jnp.int32, (rows, HALF), 1)
     sub = lax.broadcasted_iota(jnp.int32, (rows, HALF), 0)
     low = lane < LEV
-    level = lax.rem(lane, LEV)
-    floor = bottom[pl.ds(start, rows), :]
-    wet = [
-        (level < jnp.where(low, floor[:, 2 * i : 2 * i + 1], floor[:, 2 * i + 1 : 2 * i + 2])).astype(F32)
-        for i in range(2)
-    ]
+    band_lane = lax.broadcasted_iota(jnp.int32, (band, HALF), 1)
+    band_sub = lax.broadcasted_iota(jnp.int32, (band, HALF), 0)
+    band_low = band_lane < LEV
+    level = lax.rem(band_lane, LEV).astype(F32)
+    load_b.wait()
+    columns = bottom.shape[0]
+    spread_of = (
+        lax.broadcasted_iota(jnp.int32, (columns, 2 * HALF), 1) // LEV
+        == lax.broadcasted_iota(jnp.int32, (columns, 2 * HALF), 0)
+    )
+    floors[...] = lax.dot_general(
+        bottom[...].astype(F32).astype(jnp.bfloat16),
+        jnp.where(spread_of, 1.0, 0.0).astype(jnp.bfloat16),
+        (((0,), (0,)), ((), ())),
+        preferred_element_type=F32,
+    )
+    wet = []
     for i in range(2):
+        floor = floors[:, i * HALF : (i + 1) * HALF]
+        wet.append(jnp.where(level < floor, 1.0, 0.0))
         s0[3, :, i * HALF : (i + 1) * HALF] = wet[i]
 
     a = lax.broadcasted_iota(jnp.int32, (HALF, HALF), 0)
@@ -106,10 +135,12 @@
     incl = jnp.where(same & (a <= b), 1.0, 0.0).astype(jnp.bfloat16)
     excl = jnp.where(same & (a < b), 1.0, 0.0).astype(jnp.bfloat16)
 
-    expect = sum(jnp.where(flag, 1, 0) for flag in sends) + (ncomp - 1)
+    expect = sum(jnp.where(flag, 1, 0) for flag in sends + ocean_sends[:2]) + (ncomp - 1)
     pl.semaphore_wait(barrier, expect)
 
     def exchange(step, kind, state, rim, west, east, count):
+        rows = state.shape[1]
+        where = (ocean_targets, targets)[kind]
         ends = (
             (state.at[0:count, rows - 2 : rows, :], rim.at[step, 0:count, rows - 2 : rows, :]),
             (state.at[0:count, 0:2, :], rim.at[step, 0:count, 0:2, :]),
@@ -122,29 +153,46 @@
                 dst_ref=target,
                 send_sem=send_sem.at[step, kind, way],
                 recv_sem=recv_sem.at[step, kind, way],
-                device_id=targets[way],
+                device_id=where[way],
                 device_id_type=MESH,
             )
             for way, (source, target) in enumerate(ends)
         ]
 
-    def begin(copies):
+    def begin(copies, sends):
         for way in range(4):
             @pl.when(sends[way])
             def _(way=way):
                 copies[way].start()
 
-    def arrive(copies):
+    def arrive(copies, gets):
         for way in range(4):
             @pl.when(gets[way])
             def _(way=way):
                 copies[way].wait_recv()
 
-    def left(copies):
+    def left(copies, sends):
         for way in range(4):
             @pl.when(sends[way])
             def _(way=way):
                 copies[way].wait_send()
+
+    def hand_round(step, q_ref):
+        copies = [
+            pltpu.make_async_remote_copy(
+                src_ref=q_ref.at[2],
+                dst_ref=chl.at[step, mine, :],
+                send_sem=gsend_sem.at[step, k],
+                recv_sem=grecv_sem.at[step, k],
+                device_id=peer,
+                device_id_type=MESH,
+            )
+            for k, peer in enumerate(peers)
+        ]
+        for copy in copies:
+            copy.start()
+        chl[step, mine, :] = q_ref[2]
+        return copies
 
     def level_sums(parts, ladder):
         x = jnp.concatenate(parts, axis=0)
@@ -157,7 +205,8 @@
             jnp.concatenate([high, mid, last], axis=0), ladder, preferred_element_type=F32
         )
         y = y[0:n] + y[n : 2 * n] + y[2 * n : 3 * n]
-        return [y[i * rows : (i + 1) * rows] for i in range(len(parts))]
+        tall = parts[0].shape[0]
+        return [y[i * tall : (i + 1) * tall] for i in range(len(parts))]
 
     def pick(mask, x, y):
         if x.ndim == 3:
@@ -170,16 +219,17 @@
     def spin(x, shift):
         return pltpu.roll(x, shift, axis=x.ndim - 2)
 
-    first, first_two, final = sub < 1, sub < 2, sub > rows - 2
+    def edge(x, count):
+        return (sub if x.shape[-2] == rows else band_sub) < count
 
     def next_row(x, rim):
-        return spin(pick(first, rim, x), rows - 1)
+        return spin(pick(edge(x, 1), rim, x), x.shape[-2] - 1)
 
     def after_row(x, rim):
-        return spin(pick(first_two, rim, x), rows - 2)
+        return spin(pick(edge(x, 2), rim, x), x.shape[-2] - 2)
 
     def prev_row(x, rim):
-        return spin(pick(final, rim, x), 1)
+        return spin(pick(edge(x, x.shape[-2] - 1), x, rim), 1)
 
     def limited(below, middle, above, pos, sign_half, speed, q_a, q_b):
         other = pick(pos, below, above)
@@ -194,36 +244,44 @@
     copies_s = exchange(0, 0, s0, rim_s, west_s, east_s, 4)
     copies_q = exchange(0, 1, q0, rim_q, west_q, east_q, ntr)
     load_o.wait()
-    begin(copies_s)
+    begin(copies_s, ocean_sends)
     load_q.wait()
-    begin(copies_q)
-    pending = copies_s + copies_q
-    pend_s, pend_q = [copies_s], [copies_q]
-
-    states = (s0, s1, s2)
-    gathers = []
-    wet_ring = None
+    shared = hand_round(0, q0)
+    begin(copies_q, sends)
+    pend_s, pend_q, given = [copies_s], [copies_q], [shared]
+
+    def own(ref, lead, offset=0):
+        at = pl.ds(start + offset, rows)
+        return [ref[(*lead, at, slice(i * HALF, (i + 1) * HALF))] for i in range(ref.shape[-1] // HALF)]
+
+    def lay(ref, values, rims):
+        for i in range(2):
+            cols = slice(i * HALF, (i + 1) * HALF)
+            ref[0:rows, cols] = rims[i][band - rows : band]
+            ref[rows : rows + band, cols] = values[i]
+            ref[rows + band : 2 * rows + band, cols] = rims[i][0:rows]
+        here, before, beyond = own(ref, (), rows), own(ref, ()), own(ref, (), 2 * rows)
+        return here, [pick(sub < 1, y, x) for x, y in zip(before, beyond)]
+
+    load_c.wait()
     for step in range(STEPS):
-        q_ref, state, after = (q0, q1)[step], states[step], states[step + 1]
+        q_ref, state = (q0, q1)[step], (s0, s1)[step]
+        after = s1 if step + 1 < STEPS else oc_out
         u, v, temp = (halves(state, k) for k in range(3))
-        absorb = [
-            (ATTEN_WATER + ATTEN_CHL * jnp.maximum(c, 0.0)) * w
-            for c, w in zip(halves(q_ref, 2), wet)
-        ]
-        above = level_sums(absorb, excl)
-        sunlight = [jnp.exp(-x) for x in above]
-        heating = [s * (1.0 - jnp.exp(-x)) * w for s, x, w in zip(sunlight, absorb, wet)]
-
-        arrive(copies_s)
+
+        arrive(copies_s, ocean_gets)
         if step == 0:
             wet_line = [west_s[0, 3], *wet, east_s[0, 3]]
             wet_rim = halves(rim_s, 0, 3)
             turned = [swap(x) for x in wet_line]
-            col_gate = [
-                wet_line[i] * pick(low, turned[i], turned[i + 1]) for i in range(3)
-            ]
-            row_gate = [w * next_row(w, r) for w, r in zip(wet, wet_rim)]
-            rim_gate = [r * spin(w, rows - 1) for w, r in zip(wet, wet_rim)]
+            for i in range(3):
+                u_all[:, i * HALF : (i + 1) * HALF] = wet_line[i] * pick(
+                    band_low, turned[i], turned[i + 1]
+                )
+            col_gate = own(u_all, ())[:3]
+            wet_own, wet_near = lay(wet_all, wet, wet_rim)
+            row_gate = [w * next_row(w, r) for w, r in zip(wet_own, wet_near)]
+            rim_gate = [r * spin(w, rows - 1) for w, r in zip(wet_own, wet_near)]
         line = [west_s[step, 2], *temp, east_s[step, 2]]
         rim = halves(rim_s, step, 2)
         sums = level_sums(line + rim, incl)
@@ -233,14 +291,14 @@
         v_line = [west_s[step, 1], *v, east_s[step, 1]]
         new_u = []
         for i in range(4):
-            east = pick(low, turned[i], turned[min(i + 1, 3)])
-            west = pick(low, turned[max(i - 1, 0)], turned[i])
+            east = pick(band_low, turned[i], turned[min(i + 1, 3)])
+            west = pick(band_low, turned[max(i - 1, 0)], turned[i])
             slope = (0.5 * PRESSURE) * (east - west)
             new_u.append(
                 wet_line[i] * ((1.0 - DAMPING) * u_line[i] + TIME_STEP * (CORIOLIS * v_line[i] - slope))
             )
         u_rim, v_rim = halves(rim_s, step, 0), halves(rim_s, step, 1)
-        new_v, new_v_rim, new_temp = [], [], []
+        new_v, new_v_rim, new_temp, spreads = [], [], [], []
         turned = [swap(x) for x in line]
         for i in range(2):
             slope = (0.5 * PRESSURE) * (
@@ -255,38 +313,40 @@
             new_v_rim.append(
                 wet_rim[i] * ((1.0 - DAMPING) * v_rim[i] - TIME_STEP * (CORIOLIS * u_rim[i] + slope))
             )
-            spread = (
+            spreads.append(
                 next_row(temp[i], rim[i])
                 + prev_row(temp[i], rim[i])
-                + pick(low, turned[i + 1], turned[i + 2])
-                + pick(low, turned[i], turned[i + 1])
+                + pick(band_low, turned[i + 1], turned[i + 2])
+                + pick(band_low, turned[i], turned[i + 1])
                 - 4.0 * temp[i]
             )
+        for copy in shared:
+            copy.wait_recv()
+        absorb = [
+            (ATTEN_WATER + ATTEN_CHL * jnp.maximum(c, 0.0)) * w
+            for c, w in zip(halves(chl, step), wet)
+        ]
+        light = [jnp.exp(-x) for x in level_sums(absorb, excl)]
+        for i in range(2):
+            heating = light[i] * (1.0 - jnp.exp(-absorb[i])) * wet[i]
             new_temp.append(
-                wet[i] * (temp[i] + TIME_STEP * (HEAT_GAIN * heating[i] + DIFFUSE * spread))
+                wet[i] * (temp[i] + TIME_STEP * (HEAT_GAIN * heating + DIFFUSE * spreads[i]))
             )
         for i in range(2):
             cols = slice(i * HALF, (i + 1) * HALF)
             after[0, :, cols] = new_u[i + 1]
             after[1, :, cols] = new_v[i]
             after[2, :, cols] = new_temp[i]
+            sun_all[:, cols] = light[i]
         if step + 1 < STEPS:
             copies_s = exchange(step + 1, 0, after, rim_s, west_s, east_s, 3)
-            begin(copies_s)
+            begin(copies_s, ocean_sends)
             pend_s.append(copies_s)
-        else:
-            for hop in range(1, ncomp):
-                copy = pltpu.make_async_remote_copy(
-                    src_ref=after,
-                    dst_ref=band.at[:, pl.ds(start, rows), :],
-                    send_sem=gsend_sem.at[hop - 1],
-                    recv_sem=grecv_sem.at[hop - 1],
-                    device_id={"comp": lax.rem(comp + hop, ncomp)},
-                    device_id_type=MESH,
-                )
-                copy.start()
-                gathers.append(copy)
-            band[:, pl.ds(start, rows), :] = after[...]
+        for i in range(4):
+            u_all[:, i * HALF : (i + 1) * HALF] = new_u[i]
+        new_u = own(u_all, ())
+        new_v, new_v_rim = lay(v_all, new_v, new_v_rim)
+        new_temp, sunlight = own(after, (2,)), own(sun_all, ())
 
         turned = [swap(x) for x in new_u]
         col_speed = [
@@ -307,7 +367,7 @@
 
         col_gauge, row_gauge, rim_gauge = gauge(col_speed), gauge(row_speed), gauge(rim_speed)
 
-        arrive(copies_q)
+        arrive(copies_q, gets)
 
         def advect(lo, hi):
             part = slice(lo, hi)
@@ -378,29 +438,35 @@
                 dying + (1.0 - ASSIM) * grazing + GRAZER_LOSS * grazer - remineral,
             )
             for k in range(CORE):
-                put(k, k + 1, i, ((adv[k] + REACT_STEP * changes[k]) * wet[i])[None])
+                put(k, k + 1, i, ((adv[k] + REACT_STEP * changes[k]) * wet_own[i])[None])
             net.append(REACT_STEP * (growth - remineral))
+        if step + 1 < STEPS:
+            shared = hand_round(step + 1, q1)
+            given.append(shared)
         for lo in range(CORE, ntr, CHUNK):
             hi = min(lo + CHUNK, ntr)
             adv = advect(lo, hi)
             for i in range(2):
                 for k in range(lo, hi):
-                    put(k, k + 1, i, ((adv[i][k - lo] + stoich[k - CORE] * net[i]) * wet[i])[None])
+                    put(k, k + 1, i, ((adv[i][k - lo] + stoich[k - CORE] * net[i]) * wet_own[i])[None])
         if step + 1 < STEPS:
             copies_q = exchange(step + 1, 1, q1, rim_q, west_q, east_q, ntr)
-            begin(copies_q)
+            begin(copies_q, sends)
             pend_q.append(copies_q)
 
-    for copies in pend_s + pend_q:
-        left(copies)
-    for copy in gathers:
-        copy.wait()
-    oc_out[...] = band[...]
+    for copies in pend_s:
+        left(copies, ocean_sends)
+    for copies in pend_q:
+        left(copies, sends)
+    for copies in given:
+        for copy in copies:
+            copy.wait_send()
 
 
 def shards(ocean, tracers, bottom, stoich):
     ncomp, nty, ntx = (lax.axis_size(name) for name in ("comp", "ty", "tx"))
     ntr, _, rows, width = tracers.shape
+    band = ocean.shape[1]
     vmem = pl.BlockSpec(memory_space=pltpu.VMEM)
     tr_out, oc_out = pl.pallas_call(
         functools.partial(kernel, ncomp, nty, ntx),
@@ -409,35 +475,38 @@
             jax.ShapeDtypeStruct(ocean.shape, F32),
         ),
         in_specs=[
-            pl.BlockSpec(memory_space=pl.ANY),
-            pl.BlockSpec(memory_space=pl.ANY),
-            vmem,
-            pl.BlockSpec(memory_space=pltpu.SMEM),
-        ],
+            pl.BlockSpec(memory_space=pltpu.HBM),
+        ] * 4,
         out_specs=(vmem, vmem),
         scratch_shapes=[
+            pltpu.VMEM(bottom.shape[::-1], jnp.int32),
+            pltpu.SMEM(stoich.shape, F32),
+            pltpu.VMEM((bottom.shape[0], width), F32),
             pltpu.VMEM((ntr, rows, width), F32),
             pltpu.VMEM((ntr, rows, width), F32),
-            pltpu.VMEM((4, rows, width), F32),
-            pltpu.VMEM((3, rows, width), F32),
-            pltpu.VMEM((3, rows, width), F32),
-            pltpu.VMEM(ocean.shape, F32),
+            pltpu.VMEM((4, band, width), F32),
+            pltpu.VMEM((3, band, width), F32),
+            pltpu.VMEM((STEPS, band, width), F32),
+            pltpu.VMEM((band, 2 * width), F32),
+            pltpu.VMEM((band + 2 * rows, width), F32),
+            pltpu.VMEM((band + 2 * rows, width), F32),
+            pltpu.VMEM((band, width), F32),
             pltpu.VMEM((STEPS, ntr, rows, width), F32),
             pltpu.VMEM((STEPS, ntr, rows, HALF), F32),
             pltpu.VMEM((STEPS, ntr, rows, HALF), F32),
-            pltpu.VMEM((STEPS, 4, rows, width), F32),
-            pltpu.VMEM((STEPS, 4, rows, HALF), F32),
-            pltpu.VMEM((STEPS, 4, rows, HALF), F32),
-            pltpu.SemaphoreType.DMA((2,)),
+            pltpu.VMEM((STEPS, 4, band, width), F32),
+            pltpu.VMEM((STEPS, 4, band, HALF), F32),
+            pltpu.VMEM((STEPS, 4, band, HALF), F32),
+            pltpu.SemaphoreType.DMA((4,)),
             pltpu.SemaphoreType.DMA((STEPS, 2, 4)),
             pltpu.SemaphoreType.DMA((STEPS, 2, 4)),
-            pltpu.SemaphoreType.DMA((max(ncomp - 1, 1),)),
-            pltpu.SemaphoreType.DMA((max(ncomp - 1, 1),)),
+            pltpu.SemaphoreType.DMA((STEPS, max(ncomp - 1, 1))),
+            pltpu.SemaphoreType.DMA((STEPS, max(ncomp - 1, 1))),
         ],
         compiler_params=pltpu.CompilerParams(
             collective_id=0, has_side_effects=True, vmem_limit_bytes=32 * 1024 * 1024
         ),
-    )(tracers, ocean, bottom, stoich)
+    )(*(pltpu.with_memory_space_constraint(x, pltpu.HBM) for x in (tracers, ocean, bottom.T, stoich)))
     return oc_out, tr_out
 
 

time: 19.3 us -> 13.8 us (0.72)
  Pallas kernels: 14.7 us -> 11.8 us
  local copies, waits for them, and re-layouts: 3.76 us -> 1.29 us
    pallas_call x1, Pallas kernels: 14.7 us -> 11.8 us  [shards(): pl.pallas_call(functools.partial(kernel, ncomp, nty, ntx), out_shape=(jax...]
    unnamed x9 -> x2, local copies, waits for them, and re-layouts: 3.76 us -> 1.29 us
where the time goes in v2:
time: 13.8 us; the launch traced here: 13.7 us
  Pallas kernels  11.8 us (86%)
  local copies, waits for them, and re-layouts  1.29 us (9%)
  between operations  0.64 us (5%)
    pallas_call x1, Pallas kernels, shards(): pl.pallas_call(functools.partial(kernel, ncomp, nty, ntx), out_shape=(jax...  11.8 us
    unnamed x2, local copies, waits for them, and re-layouts  1.29 us

profile of v2, /device:TPU:0, one launch (start us, length us, event | category | flops | bytes accessed | tf_op | source)
XLA Modules:
  0.0 13.7 jit_solution(14922200353916828600)
XLA Ops:
  0.6 11.8 %shard_map.59 = (f32[19,1,8,256]{3,2,1,0:T(8,128)S(1)}, f32[3,16,256]{2,1,0:T(8,128)S(1)}) custom-call(f32[19,1,8,256]{3,2,1,0:T(8,128)} %tr_in.1, f32[3,16,256]{2,1,0:T(8,128)} %oc_in.1, s32[4,16]{1,0:T(4,128)} %bitcast.1, f32[14]{0:T(128)} %stoich_in.1), custom_call_target="tpu_custom_call" | custom-call | tf_op jit(solution)/shard_map/pallas_call | solution.py:471
  12.4 0.6 %copy.8 = f32[3,16,256]{2,1,0:T(8,128)} copy(f32[3,16,256]{2,1,0:T(8,128)S(1)} %get-tuple-element.8) | data formatting | bytes 98304
  13.0 0.7 %copy.9 = f32[19,1,8,256]{3,2,1,0:T(8,128)} copy(f32[19,1,8,256]{3,2,1,0:T(8,128)S(1)} %get-tuple-element.9) | data formatting | bytes 311296

commit v3 on v2

--- a/solution.py
+++ b/solution.py
@@ -89,8 +89,16 @@
     ocean_sends = (has_next, has_last, has_east, has_west)
     ocean_gets = (has_last, has_next, has_west, has_east)
 
-    for ref in (rim_q, west_q, east_q, rim_s, west_s, east_s):
-        ref[...] = jnp.zeros(ref.shape, F32)
+    def clear(missing, ref, lo, hi):
+        @pl.when(missing)
+        def _():
+            ref[:, :, lo:hi, :] = jnp.zeros((*ref.shape[:2], hi - lo, ref.shape[3]), F32)
+
+    for ref, above, below in ((rim_q, has_up, has_down), (rim_s, ty > 0, ty < nty - 1)):
+        clear(jnp.logical_not(above), ref, ref.shape[2] - 2, ref.shape[2])
+        clear(jnp.logical_not(below), ref, 0, 2)
+    for ref, there in ((west_q, has_west), (west_s, has_west), (east_q, has_east), (east_s, has_east)):
+        clear(jnp.logical_not(there), ref, 0, ref.shape[2])
 
     barrier = pltpu.get_barrier_semaphore()
     for way in range(4):
@@ -103,6 +111,10 @@
             pl.semaphore_signal(barrier, inc=1, device_id=ocean_targets[way], device_id_type=MESH)
     for peer in peers:
         pl.semaphore_signal(barrier, inc=1, device_id=peer, device_id_type=MESH)
+
+    for ref in (rim_q, rim_s):
+        inside = ref.shape[2] - 4
+        ref[:, :, 2 : 2 + inside, :] = jnp.zeros((*ref.shape[:2], inside, ref.shape[3]), F32)
 
     lane = lax.broadcasted_iota(jnp.int32, (rows, HALF), 1)
     sub = lax.broadcasted_iota(jnp.int32, (rows, HALF), 0)

time: 13.8 us -> 13.9 us (level)
  no operation moved by 1% of the time
where the time goes in v3:
time: 13.9 us; the launch traced here: 13.7 us
  Pallas kernels  11.8 us (85%)
  local copies, waits for them, and re-layouts  1.29 us (9%)
  between operations  0.64 us (5%)
    pallas_call x1, Pallas kernels, shards(): pl.pallas_call(functools.partial(kernel, ncomp, nty, ntx), out_shape=(jax...  11.8 us
    unnamed x2, local copies, waits for them, and re-layouts  1.29 us

profile of v3, /device:TPU:0, one launch (start us, length us, event | category | flops | bytes accessed | tf_op | source)
XLA Modules:
  0.0 13.7 jit_solution(15598392461290100978)
XLA Ops:
  0.6 11.8 %shard_map.59 = (f32[19,1,8,256]{3,2,1,0:T(8,128)S(1)}, f32[3,16,256]{2,1,0:T(8,128)S(1)}) custom-call(f32[19,1,8,256]{3,2,1,0:T(8,128)} %tr_in.1, f32[3,16,256]{2,1,0:T(8,128)} %oc_in.1, s32[4,16]{1,0:T(4,128)} %bitcast.1, f32[14]{0:T(128)} %stoich_in.1), custom_call_target="tpu_custom_call" | custom-call | tf_op jit(solution)/shard_map/pallas_call | solution.py:483
  12.4 0.6 %copy.8 = f32[3,16,256]{2,1,0:T(8,128)} copy(f32[3,16,256]{2,1,0:T(8,128)S(1)} %get-tuple-element.8) | data formatting | bytes 98304
  13.0 0.7 %copy.9 = f32[19,1,8,256]{3,2,1,0:T(8,128)} copy(f32[19,1,8,256]{3,2,1,0:T(8,128)S(1)} %get-tuple-element.9) | data formatting | bytes 311296
